TPU v7x, 32 devices: a whole 2x2x4 slice. The times are simulated.
32 devices in a mesh: grp: 2 (over y), space: 4 (over z), chaos: 2 (over x), mode: 2 (over core).
Axes of the slice: x: 2, y: 2, z: 4, core: 2. Of those that a mesh axis runs over, the one named last changes fastest.
Arguments:
- coeffs: bfloat16 [8, 48, 16384], P(None, 'chaos', ('grp', 'space')), parts along dimension 2, may hold values from -6 to 6
- tangent: bfloat16 [8, 128, 3, 128, 128], P('mode', ('grp', 'space')), parts along dimension 1, may hold values from -0.3125 to 0.3125
- block_cols: int32 [128, 3], P(('grp', 'space')), parts along dimension 0, may hold values from 0 to 63, as said below
- galerkin: float32 [8, 48, 48], replicated, may hold values from -2.5 to 3
- galerkin_mask: int32 [8, 48, 48], replicated, may hold values 0 or 1
Outputs:
- applied: bfloat16 [8, 48, 16384], P(None, ('chaos', 'mode'), ('grp', 'space')), parts along dimension 2
There are 2 independent parts, one for each index of `grp`. A program takes and returns all parts, laid end to end along the dimension named above; an argument that names none is the same for every part. Nothing has to cross between parts.
Inputs may be any that keep to these rules, and one draw needn't show every extreme that they name: `block_cols`: each row holds its own block index first, then two other block indices at cyclic distance 1 or 2 from it (modulo 64); the three are distinct.
All inputs are finite; a program needn't handle non-finite values.
Results may differ from a plain program's by a relative error of at most 0.001.
Values may be sent and summed in bfloat16 or wider, within the bound.
A program may use at most 192 MiB of HBM per device.

v0:
```python
import jax
import jax.numpy as jnp
from jax import lax
from jax.sharding import PartitionSpec as P

REACH = 2


def from_behind(x, axis, by):
    size = lax.axis_size(axis)
    return lax.ppermute(x, axis, [(i, (i + by) % size) for i in range(size)])


def per_device(coeffs, tangent, block_cols, galerkin, galerkin_mask):
    field_count, rows_in, tile_dofs = coeffs.shape
    mode_count, block_rows, slot_count, block_size, _ = tangent.shape
    first = lax.broadcasted_iota(jnp.int32, galerkin.shape, 1)
    second = lax.broadcasted_iota(jnp.int32, galerkin.shape, 2)
    keep = (first == second) | (galerkin_mask == 1)
    mixing = jnp.where(keep, galerkin, jnp.zeros_like(galerkin))
    local_mix = lax.dynamic_slice_in_dim(mixing, lax.axis_index("mode") * mode_count, mode_count, 0)
    span_blocks = block_rows + 2 * REACH
    shell_blocks = block_rows * lax.axis_size("space")
    global_rows = lax.axis_index("space") * block_rows + jnp.arange(block_rows, dtype=jnp.int32)
    offsets = (block_cols - global_rows[:, None] + shell_blocks + REACH) % shell_blocks - REACH
    position = jnp.arange(block_rows, dtype=jnp.int32)[:, None] + offsets + REACH
    onehot = (
        position[:, :, None] == jnp.arange(span_blocks, dtype=jnp.int32)[None, None, :]
    ).astype(jnp.float32)
    count = coeffs.shape[1]
    pieces = coeffs.reshape(field_count, count, block_rows, block_size)
    contrib = jnp.einsum("fqrb,krnbc->kfqrnc", pieces, tangent, preferred_element_type=jnp.float32)
    placed = jnp.einsum("kfqrnc,rnj->kfqjc", contrib, onehot, precision=lax.Precision.HIGHEST)
    own_image = placed.reshape(mode_count, field_count, count, span_blocks * block_size)
    own_mix = lax.dynamic_slice_in_dim(local_mix, lax.axis_index("chaos") * rows_in, rows_in, 1)
    summed = lax.psum_scatter(
        jnp.einsum("kqp,kfqx->pfx", own_mix, own_image, precision=lax.Precision.HIGHEST),
        ("chaos", "mode"),
        scatter_dimension=0,
        tiled=True,
    )
    rim_width = REACH * block_size
    lower_rim = summed[:, :, :rim_width]
    upper_rim = summed[:, :, rim_width + tile_dofs :]
    center = summed[:, :, rim_width : rim_width + tile_dofs]
    from_below = from_behind(upper_rim, "space", 1)
    from_above = from_behind(lower_rim, "space", -1)
    center = center.at[:, :, :rim_width].add(from_below)
    center = center.at[:, :, tile_dofs - rim_width :].add(from_above)
    return jnp.transpose(center, (1, 0, 2)).astype(jnp.bfloat16)


def solution(mesh):
    return jax.shard_map(
        per_device,
        mesh=mesh,
        in_specs=(
            P(None, "chaos", ("grp", "space")),
            P("mode", ("grp", "space"), None, None, None),
            P(("grp", "space"), None),
            P(),
            P(),
        ),
        out_specs=P(None, ("chaos", "mode"), ("grp", "space")),
        check_vma=False,
    )
```

profile of v0, /device:TPU:0, one launch (start us, length us, event | category | flops | bytes accessed | tf_op | source)
XLA Modules:
  0.0 127.5 jit_solution(18002118536908534599)
XLA Ops:
  6.5 0.0 reduce-scatter.2.cloned.1.call-start
  6.5 1.3 %copy.24 = bf16[24,8,16,128]{3,2,1,0:T(8,128)(2,1)S(1)} copy(bf16[24,8,16,128]{3,1,2,0:T(8,128)(2,1)} %bitcast.38) | data formatting | bytes 1572864
  7.8 0.1 bitcast_bitcast_fusion
  8.0 0.0 copy-start
  8.0 11.8 %convolution_bitcast_fusion = f32[4,8,24,16,3,128]{5,2,1,4,0,3:T(8,128)} fusion(bf16[8,24,16,128,1,1]{3,2,1,0,5,4:T(8,128)(2,1)S(1)} %bitcast_bitcast_fusion, bf16[4,16,3,128,128]{4,3,2,1,0:T(8,128)(2,1)} %param.10), kind=kOutput, calls=%fused_computation.2 | convolution fusion | flops 1207959552 | bytes 25952256 | tf_op jit(solution)/shard_map/fqrb,krnbc->kfqrnc/dot_general | solution.py:32
  19.8 0.0 copy-done
  19.9 25.3 %fusion.3 = f32[4,8,24,20,128]{4,3,2,1,0:T(8,128)} fusion(f32[4,8,24,16,3,128]{5,2,1,4,0,3:T(8,128)} %convolution_bitcast_fusion, s32[16,3]{0,1:T(4,128)S(1)} %fusion.22), kind=kOutput, calls=%fused_computation.5 | convolution fusion | flops 1132463104 | bytes 26738880 | tf_op jit(solution)/shard_map/kfqrnc,rnj->kfqjc/dot_general | solution.py:33
  45.2 9.3 %reshape.72 = f32[4,8,24,2560]{3,2,1,0:T(8,128)} reshape(f32[4,8,24,20,128]{4,3,2,1,0:T(8,128)} %fusion.3) | data formatting | bytes 15728640 | tf_op jit(solution)/shard_map/reshape | solution.py:34
  54.4 6.2 %convolution_bitcast_fusion.1 = f32[48,8,2560]{2,0,1:T(8,128)S(1)} fusion(f32[4,8,24,2560]{3,2,1,0:T(8,128)} %reshape.72, f32[8,48,48]{2,1,0:T(8,128)} %param.12, s32[]{:T(128)S(6)} %select_n.23, s32[]{:T(128)S(6)} %select_n.25, s32[8,48,48]{2,1,0:T(8,128)} %param.13), kind=kOutput, calls=%fused_computation.4 | convolution fusion | flops 1132485120 | bytes 11896320 | tf_op jit(solution)/shard_map/kqp,kfqx->pfx/dot_general | solution.py:37
  60.7 4.1 %copy.14 = f32[48,8,2560]{2,1,0:T(8,128)} copy(f32[48,8,2560]{2,0,1:T(8,128)S(1)} %convolution_bitcast_fusion.1) | data formatting | bytes 7864320 | tf_op jit(solution)/shard_map/kqp,kfqx->pfx/dot_general | solution.py:37
  64.8 0.0 reduce-scatter.2.cloned.1.call-update
  64.8 45.7 %reduce-scatter.2.cloned.1.call-done = f32[12,8,2560]{2,1,0:T(8,128)} async-done(((f32[48,8,2560]{2,1,0:T(8,128)}), f32[12,8,2560]{2,1,0:T(8,128)}) %reduce-scatter.2.cloned.1.call-update) | async-done | bytes 983056 | tf_op jit(solution)/shard_map/reduce_scatter | solution.py:36
  110.5 1.0 fusion.26
  111.5 1.5 %collective-permute-start = (f32[12,8,256]{2,1,0:T(8,128)S(1)}, f32[12,8,256]{2,1,0:T(8,128)S(1)}, u32[]{:S(2)}, u32[]{:S(2)}) collective-permute-start(f32[12,8,256]{2,1,0:T(8,128)S(1)} %get-tuple-element.30), channel_id=1, source_target_pairs={{0,4},{4,8},{8,12},{12,0},{1,5},{5,9},{9,13},{13,1},{2,6},{6,10},{... | collective-permute-start | bytes 294920 | tf_op jit(solution)/shard_map/ppermute | solution.py:11
  113.0 2.3 %collective-permute-start.1 = (f32[12,8,256]{2,1,0:T(8,128)S(1)}, f32[12,8,256]{2,1,0:T(8,128)S(1)}, u32[]{:S(2)}, u32[]{:S(2)}) collective-permute-start(f32[12,8,256]{2,1,0:T(8,128)S(1)} %get-tuple-element.29), channel_id=1, source_target_pairs={{0,12},{4,0},{8,4},{12,8},{1,13},{5,1},{9,5},{13,9},{2,14},{6,2},{... | collective-permute-start | bytes 294920 | tf_op jit(solution)/shard_map/ppermute | solution.py:11
  115.3 1.2 slice.63
  116.5 2.3 %collective-permute-done = f32[12,8,256]{2,1,0:T(8,128)S(1)} collective-permute-done((f32[12,8,256]{2,1,0:T(8,128)S(1)}, f32[12,8,256]{2,1,0:T(8,128)S(1)}, u32[]{:S(2)}, u32[]{:S(2)}) %collective-permute-start) | collective-permute-done | bytes 98336 | tf_op jit(solution)/shard_map/ppermute | solution.py:11
  118.9 0.9 fusion.8
  119.8 0.0 collective-permute-done.1
  119.8 0.8 convert_bitcast_fusion
  (3 shorter events, 0.0 us)
Async XLA Ops:
  6.5 104.0 %reduce-scatter.2.cloned.1.call-start = ((), (), s32[]{:S(2)}) async-start(), calls=%async_computation.1 | async-start | bytes 4915200 | tf_op jit(solution)/shard_map/reduce_scatter | solution.py:36
  8.0 11.8 %copy-start = (s32[16,3]{0,1:T(4,128)S(1)}, s32[16,3]{0,1:T(4,128)}, u32[]{:S(2)}) copy-start(s32[16,3]{0,1:T(4,128)} %param.11) | copy-start | bytes 580
  111.5 7.4 %collective-permute-start = (f32[12,8,256]{2,1,0:T(8,128)S(1)}, f32[12,8,256]{2,1,0:T(8,128)S(1)}, u32[]{:S(2)}, u32[]{:S(2)}) collective-permute-start(f32[12,8,256]{2,1,0:T(8,128)S(1)} %get-tuple-element.30), channel_id=1, source_target_pairs={{0,4},{4,8},{8,12},{12,0},{1,5},{5,9},{9,13},{13,1},{2,6},{6,10},{... | collective-permute-start | bytes 294920 | tf_op jit(solution)/shard_map/ppermute | solution.py:11
  113.0 6.8 %collective-permute-start.1 = (f32[12,8,256]{2,1,0:T(8,128)S(1)}, f32[12,8,256]{2,1,0:T(8,128)S(1)}, u32[]{:S(2)}, u32[]{:S(2)}) collective-permute-start(f32[12,8,256]{2,1,0:T(8,128)S(1)} %get-tuple-element.29), channel_id=1, source_target_pairs={{0,12},{4,0},{8,4},{12,8},{1,13},{5,1},{9,5},{13,9},{2,14},{6,2},{... | collective-permute-start | bytes 294920 | tf_op jit(solution)/shard_map/ppermute | solution.py:11
Sparse Core Ops, SparseCore 0:
  64.9 45.5 reduce-scatter.1
where the time goes:
time: 128 us; the launch traced here: 127 us
  waiting for transfers between devices  48.1 us (38%)
  matrix products  43.4 us (34%)
  local copies, waits for them, and re-layouts  17 us (13%)
  between operations  13.5 us (11%)
  starting transfers between devices  3.88 us (3%)
  other arithmetic  1.74 us (1%)
    reduce_scatter x1, waiting for transfers between devices, per_device(): lax.psum_scatter(jnp.einsum('kqp,kfqx->pfx', own_mix, own_image, precisio...  45.7 us
    dot_general x1, matrix products, per_device(): jnp.einsum('kfqrnc,rnj->kfqjc', contrib, onehot, precision=lax.Precision....  25.3 us
    dot_general x1, matrix products, per_device(): jnp.einsum('fqrb,krnbc->kfqrnc', pieces, tangent, preferred_element_type=...  11.8 us
    reshape x1, local copies, waits for them, and re-layouts, per_device(): placed.reshape(mode_count, field_count, count, span_blocks * block_size)  9.25 us
    dot_general x1, matrix products, per_device(): jnp.einsum('kqp,kfqx->pfx', own_mix, own_image, precision=lax.Precision.H...  6.23 us
    dot_general x1, local copies, waits for them, and re-layouts, per_device(): jnp.einsum('kqp,kfqx->pfx', own_mix, own_image, precision=lax.Precision.H...  4.13 us
    ppermute x2, starting transfers between devices, from_behind(): return lax.ppermute(x, axis, [(i, (i + by) % size) for i in range(size)])  3.88 us
  transfers between devices with their start and end apart: 3, of which 2 were waited for; matrix products, arithmetic and copies ran while one was open for 2% of the time, Pallas kernels for 0%

commit v1 on v0

v1 whole, which is shorter than its diff:
```python
import functools

import jax
import jax.numpy as jnp
import numpy as np
from jax import lax
from jax.experimental import pallas as pl
from jax.experimental.pallas import tpu as pltpu
from jax.sharding import PartitionSpec as P

REACH = 2
MESH = pl.DeviceIdType.MESH
F32 = jnp.float32
BF16 = jnp.bfloat16


def group_of(fields, rows_in, own_p):
    for group in range(1, fields + 1):
        if fields % group == 0 and group * rows_in % 16 == 0 and group * own_p % 8 == 0:
            return group
    return fields


def kernel(dims, cols_ref, x_hbm, t_hbm, g_hbm, gm_hbm, spread_ref, same_ref, half_ref, place_ref, perm_ref,
           out_ref, x_all, t_all, g_all, gm_all, mix, z, contrib, part, recv, rim, halo,
           local_sem, xs, xr, fs, fr, ys, yr, hs, hr):
    n, space_size, fields, rows_in, own_p, group, modes, block_rows, slots, blk = dims
    chaos = lax.axis_index("chaos")
    mode = lax.axis_index("mode")
    space = lax.axis_index("space")
    other = 1 - mode
    above = lax.rem(space + 1, space_size)
    below = lax.rem(space + space_size - 1, space_size)
    span = block_rows + 2 * REACH
    chunks = block_rows // 2
    pairs = span // 2
    rows = fields * own_p
    p_size = n * rows_in
    shell = block_rows * space_size
    zero_at = block_rows * slots

    locals_ = [
        pltpu.make_async_copy(g_hbm.at[pl.ds(mode * modes, modes)], g_all, local_sem.at[0]),
        pltpu.make_async_copy(gm_hbm.at[pl.ds(mode * modes, modes)], gm_all, local_sem.at[1]),
        pltpu.make_async_copy(x_hbm, x_all.at[chaos], local_sem.at[2]),
    ]
    for k in range(modes):
        for s in range(slots):
            locals_.append(pltpu.make_async_copy(
                t_hbm.at[k, :, s],
                t_all.at[:, pl.ds(k * blk, blk), pl.ds(s * blk, blk)],
                local_sem.at[3 + k * slots + s],
            ))

    barrier = pltpu.get_barrier_semaphore()
    for d in range(1, n):
        pl.semaphore_signal(barrier, inc=1, device_id={"chaos": lax.rem(chaos + d, n)}, device_id_type=MESH)
    pl.semaphore_signal(barrier, inc=1, device_id={"mode": other}, device_id_type=MESH)
    pl.semaphore_signal(barrier, inc=1, device_id={"space": above}, device_id_type=MESH)
    pl.semaphore_signal(barrier, inc=1, device_id={"space": below}, device_id_type=MESH)
    for copy in locals_:
        copy.start()
    pl.semaphore_wait(barrier, n + 2)

    def first_row(i):
        return lax.rem(2 * i + block_rows - 2, block_rows)

    def send_x(i, d):
        cols = pl.ds(pl.multiple_of((first_row(i) + mode) * blk, blk), blk)
        return pltpu.make_async_remote_copy(
            src_ref=x_hbm.at[:, cols], dst_ref=x_all.at[chaos, :, cols],
            send_sem=xs.at[d - 1, i], recv_sem=xr.at[d - 1, i],
            device_id={"chaos": lax.rem(chaos + d, n)}, device_id_type=MESH)

    def got_x(i, d):
        source = lax.rem(chaos + n - d, n)
        cols = pl.ds(pl.multiple_of((first_row(i) + mode) * blk, blk), blk)
        return pltpu.make_async_remote_copy(
            src_ref=x_hbm.at[:, cols], dst_ref=x_all.at[source, :, cols],
            send_sem=xs.at[d - 1, i], recv_sem=xr.at[d - 1, i],
            device_id={"chaos": lax.rem(chaos + d, n)}, device_id_type=MESH)

    def forward(i, d, which):
        source = lax.rem(chaos + n - d, n)
        cols = pl.ds(pl.multiple_of((first_row(i) + which) * blk, blk), blk)
        return pltpu.make_async_remote_copy(
            src_ref=x_all.at[source, :, cols], dst_ref=x_all.at[source, :, cols],
            send_sem=fs.at[d - 1, i], recv_sem=fr.at[d - 1, i],
            device_id={"mode": other}, device_id_type=MESH)

    def first_column(q):
        return lax.rem(2 * q + span - 2, span)

    def exchange(q):
        at = pl.ds(first_column(q), 2)
        return pltpu.make_async_remote_copy(
            src_ref=part.at[at, pl.ds(rows, rows)], dst_ref=recv.at[at],
            send_sem=ys.at[q], recv_sem=yr.at[q],
            device_id={"mode": other}, device_id_type=MESH)

    def send_rim(q):
        return pltpu.make_async_remote_copy(
            src_ref=rim.at[q], dst_ref=halo.at[q],
            send_sem=hs.at[q], recv_sem=hr.at[q],
            device_id={"space": above if q == 0 else below}, device_id_type=MESH)

    def start_x(i, carry):
        for d in range(1, n):
            send_x(i, d).start()
        return carry

    lax.fori_loop(0, chunks, start_x, 0)

    locals_[0].wait()
    locals_[1].wait()
    size_r = 2 * group * own_p
    half = half_ref[...]
    target = (2 * chaos + half * (1 - 2 * mode) + mode) * own_p + place_ref[...]
    pick = (lax.broadcasted_iota(jnp.int32, (size_r, p_size), 1) == target).astype(F32).astype(BF16)
    nt = (((1,), (1,)), ((), ()))
    for k in range(modes):
        first = lax.broadcasted_iota(jnp.int32, (p_size, p_size), 0)
        second = lax.broadcasted_iota(jnp.int32, (p_size, p_size), 1)
        value = jnp.where((first == second) | (gm_all[k] == 1), g_all[k], 0.0)
        hi = value.astype(BF16)
        lo = (value - hi.astype(F32)).astype(BF16)
        hi = lax.dot_general(pick, hi, nt, preferred_element_type=F32).astype(BF16)
        lo = lax.dot_general(pick, lo, nt, preferred_element_type=F32).astype(BF16)
        both = (jnp.dot(hi, spread_ref[0], preferred_element_type=F32)
                + jnp.dot(lo, spread_ref[1], preferred_element_type=F32))
        mix[pl.ds(k * size_r, size_r), :] = (both * same_ref[...]).astype(BF16)
    contrib[zero_at] = jnp.zeros((2 * rows, blk), F32)
    for copy in locals_[2:]:
        copy.wait()

    def compute(i):
        r0 = first_row(i)
        cols = pl.ds(pl.multiple_of(r0 * blk, 2 * blk), 2 * blk)
        operator = mix[...]
        pieces = []
        for g in range(fields // group):
            at = pl.ds(g * group * rows_in, group * rows_in)
            x = [x_all[s, at, cols] for s in range(n)]
            pieces.append(jnp.dot(operator, jnp.concatenate(x + x, axis=0), preferred_element_type=F32))
        part_rows = group * own_p
        for k in range(modes):
            value = jnp.concatenate([
                piece[k * size_r + h * part_rows:k * size_r + (h + 1) * part_rows]
                for h in range(2) for piece in pieces], axis=0)
            hi = value.astype(BF16)
            lo = (value - hi.astype(F32)).astype(BF16)
            for b in range(2):
                z[b, 0:2 * rows, k * blk:(k + 1) * blk] = hi[:, b * blk:(b + 1) * blk]
                z[b, 2 * rows:4 * rows, k * blk:(k + 1) * blk] = lo[:, b * blk:(b + 1) * blk]
        for b in range(2):
            res = jnp.dot(z[b], t_all[r0 + b], preferred_element_type=F32)
            res = res[:2 * rows] + res[2 * rows:]
            for s in range(slots):
                contrib[(r0 + b) * slots + s] = res[:, s * blk:(s + 1) * blk]

    def combine(q):
        j0 = first_column(q)
        for e in range(2):
            column = j0 + e - REACH
            total = None
            for o in range(-REACH, REACH + 1):
                r = column - o
                inside = (r >= 0) & (r < block_rows)
                rc = jnp.clip(r, 0, block_rows - 1)
                if o == 0:
                    found = rc * slots
                else:
                    found = zero_at
                    for s in range(1, slots):
                        offset = lax.rem(cols_ref[rc, s] - (space * block_rows + rc) + shell + REACH, shell) - REACH
                        found = jnp.where(offset == o, rc * slots + s, found)
                term = contrib[jnp.where(inside, found, zero_at)]
                total = term if total is None else total + term
            part[j0 + e] = total
        exchange(q).start()

    def summed(j):
        return part[j, 0:rows] + recv[j]

    def store(column, value):
        value = jnp.dot(perm_ref[...], value.astype(BF16), preferred_element_type=F32)
        start = column * blk
        if not isinstance(start, int):
            start = pl.multiple_of(start, blk)
        out_ref[:, pl.ds(start, blk)] = value.astype(BF16)

    def finish(q):
        exchange(q).wait()
        j0 = first_column(q)
        for e in range(2):
            store(j0 + e - REACH, summed(j0 + e))

    def finish_rim(q):
        exchange(q).wait()
        j0 = (2 * q + span - 2) % span
        for e in range(2):
            rim[q, e] = summed(j0 + e)
        send_rim(q).start()

    def step(t, carry):
        @pl.when(t < chunks)
        def _():
            for d in range(1, n):
                got_x(t, d).wait_recv()
                forward(t, d, mode).start()

        @pl.when(t >= 1)
        def _():
            for d in range(1, n):
                forward(t - 1, d, other).wait_recv()
            compute(t - 1)
            combine(t - 1)

        @pl.when(t == 2)
        def _():
            finish_rim(0)

        @pl.when(t == 3)
        def _():
            finish_rim(1)

        @pl.when(t >= 5)
        def _():
            finish(t - 2)
        return carry

    lax.fori_loop(0, chunks + 1, step, 0)
    combine(chunks)
    combine(chunks + 1)
    for q in range(chunks - 1, chunks + 1):
        finish(q)
    exchange(2).wait()
    send_rim(0).wait()
    for e in range(2):
        store(e, summed(REACH + e) + halo[0, e])
    exchange(chunks + 1).wait()
    send_rim(1).wait()
    for e in range(2):
        store(block_rows - 2 + e, summed(block_rows + e) + halo[1, e])

    def drain(i, carry):
        for d in range(1, n):
            send_x(i, d).wait_send()
            forward(i, d, mode).wait_send()
        return carry

    lax.fori_loop(0, chunks, drain, 0)


def per_device(n, space_size, coeffs, tangent, block_cols, galerkin, galerkin_mask):
    fields, rows_in, tile = coeffs.shape
    modes, block_rows, slots, blk, _ = tangent.shape
    p_size = galerkin.shape[1]
    own_p = p_size // (2 * n)
    group = group_of(fields, rows_in, own_p)
    rows = fields * own_p
    width = n * group * rows_in
    span = block_rows + 2 * REACH
    chunks = block_rows // 2
    size_r = 2 * group * own_p

    src, fld, q = np.meshgrid(np.arange(n), np.arange(group), np.arange(rows_in), indexing="ij")
    q_of = (src * rows_in + q).reshape(-1)
    one = (np.arange(p_size)[:, None] == q_of[None, :]).astype(np.float32)
    nil = np.zeros_like(one)
    spread = jnp.asarray(np.stack([np.concatenate([one, nil], 1), np.concatenate([nil, one], 1)]), BF16)
    h_of, f_of, p_of = (a.reshape(-1) for a in np.meshgrid(np.arange(2), np.arange(group), np.arange(own_p), indexing="ij"))
    same = jnp.asarray((f_of[:, None] == np.tile(fld.reshape(-1), 2)[None, :]).astype(np.float32))
    half = jnp.asarray(np.repeat(h_of[:, None], p_size, 1).astype(np.int32))
    place = jnp.asarray(np.repeat(p_of[:, None], p_size, 1).astype(np.int32))
    to = np.arange(rows)
    source = (to % fields) * own_p + to // fields
    perm = jnp.asarray((source[:, None] == np.arange(rows)[None, :]).astype(np.float32), BF16)

    dims = (n, space_size, fields, rows_in, own_p, group, modes, block_rows, slots, blk)
    any_ = pl.BlockSpec(memory_space=pl.ANY)
    vmem = pl.BlockSpec(memory_space=pltpu.VMEM)
    out = pl.pallas_call(
        functools.partial(kernel, dims),
        out_shape=jax.ShapeDtypeStruct((rows, tile), BF16),
        in_specs=[pl.BlockSpec(memory_space=pltpu.SMEM), any_, any_, any_, any_, vmem, vmem, vmem, vmem, vmem],
        out_specs=vmem,
        scratch_shapes=[
            pltpu.VMEM((n, fields * rows_in, tile), BF16),
            pltpu.VMEM((block_rows, modes * blk, slots * blk), BF16),
            pltpu.VMEM((modes, p_size, p_size), F32),
            pltpu.VMEM((modes, p_size, p_size), jnp.int32),
            pltpu.VMEM((modes * size_r, 2 * width), BF16),
            pltpu.VMEM((2, 4 * rows, modes * blk), BF16),
            pltpu.VMEM((block_rows * slots + 1, 2 * rows, blk), F32),
            pltpu.VMEM((span, 2 * rows, blk), F32),
            pltpu.VMEM((span, rows, blk), F32),
            pltpu.VMEM((2, REACH, rows, blk), F32),
            pltpu.VMEM((2, REACH, rows, blk), F32),
            pltpu.SemaphoreType.DMA((3 + modes * slots,)),
            pltpu.SemaphoreType.DMA((n - 1, chunks)),
            pltpu.SemaphoreType.DMA((n - 1, chunks)),
            pltpu.SemaphoreType.DMA((n - 1, chunks)),
            pltpu.SemaphoreType.DMA((n - 1, chunks)),
            pltpu.SemaphoreType.DMA((chunks + 2,)),
            pltpu.SemaphoreType.DMA((chunks + 2,)),
            pltpu.SemaphoreType.DMA((2,)),
            pltpu.SemaphoreType.DMA((2,)),
        ],
        compiler_params=pltpu.CompilerParams(
            collective_id=0, has_side_effects=True, vmem_limit_bytes=48 * 1024 * 1024),
    )(block_cols, coeffs.reshape(fields * rows_in, tile), tangent, galerkin, galerkin_mask,
      spread, same, half, place, perm)
    return jnp.transpose(out.reshape(own_p, fields, tile), (1, 0, 2))


def solution(mesh):
    return jax.shard_map(
        functools.partial(per_device, mesh.shape["chaos"], mesh.shape["space"]),
        mesh=mesh,
        in_specs=(
            P(None, "chaos", ("grp", "space")),
            P("mode", ("grp", "space"), None, None, None),
            P(("grp", "space"), None),
            P(),
            P(),
        ),
        out_specs=P(None, ("chaos", "mode"), ("grp", "space")),
        check_vma=False,
    )
```

time: 128 us -> 30.3 us (0.24)
  waiting for transfers between devices: 48.1 us -> 0 us
  matrix products: 43.4 us -> 0 us
  Pallas kernels: 0 us -> 21.5 us
  between operations: 13.5 us -> 0.02 us
  local copies, waits for them, and re-layouts: 17 us -> 8.3 us
  starting transfers between devices: 3.88 us -> 0 us
  other arithmetic: 1.74 us -> 0 us
    reduce_scatter x1 -> x0, waiting for transfers between devices: 45.7 us -> none  [per_device(): lax.psum_scatter(jnp.einsum('kqp,kfqx->pfx', own_mix, own_image, precisio...]
    dot_general x3 -> x0, matrix products: 43.4 us -> none  [the longest x1 25.3 us: per_device(): jnp.einsum('kfqrnc,rnj->kfqjc', contrib, onehot, precision=lax.Precision....]
    pallas_call x0 -> x1, Pallas kernels: none -> 21.5 us  [per_device(): pl.pallas_call(functools.partial(kernel, dims), out_shape=jax.ShapeDtypeS...]
    reshape x2 -> x0, local copies, waits for them, and re-layouts: 9.39 us -> none  [the longest x1 9.25 us: per_device(): placed.reshape(mode_count, field_count, count, span_blocks * block_size)]
    unnamed x3 -> x18, local copies, waits for them, and re-layouts: 1.29 us -> 8.3 us
    dot_general x1 -> x0, local copies, waits for them, and re-layouts: 4.13 us -> none  [per_device(): jnp.einsum('kqp,kfqx->pfx', own_mix, own_image, precision=lax.Precision.H...]
    ppermute x2 -> x0, starting transfers between devices: 3.88 us -> none  [from_behind(): return lax.ppermute(x, axis, [(i, (i + by) % size) for i in range(size)])]
    ppermute x2 -> x0, waiting for transfers between devices: 2.34 us -> none  [from_behind(): return lax.ppermute(x, axis, [(i, (i + by) % size) for i in range(size)])]
  transfers between devices with their start and end apart: 3 -> 0, of which waited for: 2 -> 0; matrix products, arithmetic and copies ran while one was open for 2% -> 0% of each run, Pallas kernels for 0% -> 0%
where the time goes in v1:
time: 30.3 us; the launch traced here: 29.8 us
  Pallas kernels  21.5 us (71%)
  local copies, waits for them, and re-layouts  8.3 us (27%)
    pallas_call x1, Pallas kernels, per_device(): pl.pallas_call(functools.partial(kernel, dims), out_shape=jax.ShapeDtypeS...  21.5 us
    unnamed x18, local copies, waits for them, and re-layouts  8.3 us

profile of v1, /device:TPU:0, one launch (start us, length us, event | category | flops | bytes accessed | tf_op | source)
XLA Modules:
  0.0 29.8 jit_solution(4398509131021960441)
XLA Ops:
  0.0 0.8 %copy.11.cols_ref = s32[16,3]{1,0:T(8,128)S(1)} copy(s32[16,3]{0,1:T(4,128)} %param.12) | data formatting | bytes 384 | tf_op args[2]
  0.8 0.0 copy-start
  0.8 1.1 %copy-done = bf16[8,24,2048]{2,1,0:T(8,128)(2,1)S(1)} copy-done((bf16[8,24,2048]{2,1,0:T(8,128)(2,1)S(1)}, bf16[8,24,2048]{2,1,0:T(8,128)(2,1)}, u32[]{:S(2)}) %copy-start) | copy-done | bytes 786456
  1.9 0.0 copy-start.1
  1.9 0.9 %copy-done.1 = f32[8,48,48]{2,1,0:T(8,128)S(1)} copy-done((f32[8,48,48]{2,1,0:T(8,128)S(1)}, f32[8,48,48]{2,1,0:T(8,128)}, u32[]{:S(2)}) %copy-start.1) | copy-done | bytes 73752
  2.8 0.0 copy-start.2
  2.8 0.9 %copy-done.2 = s32[8,48,48]{2,1,0:T(8,128)S(1)} copy-done((s32[8,48,48]{2,1,0:T(8,128)S(1)}, s32[8,48,48]{2,1,0:T(8,128)}, u32[]{:S(2)}) %copy-start.2) | copy-done | bytes 73752
  3.7 0.0 copy-start.3
  3.7 0.8 %copy-done.3 = f32[48,192]{1,0:T(8,128)S(1)} copy-done((f32[48,192]{1,0:T(8,128)S(1)}, f32[48,192]{1,0:T(8,128)}, u32[]{:S(2)}) %copy-start.3) | copy-done | bytes 36888
  4.5 0.0 copy-start.4
  4.5 0.8 %copy-done.4 = bf16[2,48,192]{2,1,0:T(8,128)(2,1)S(1)} copy-done((bf16[2,48,192]{2,1,0:T(8,128)(2,1)S(1)}, bf16[2,48,192]{2,1,0:T(8,128)(2,1)}, u32[]{:S(2)}) %copy-start.4) | copy-done | bytes 36888
  5.3 0.0 copy-start.5
  5.3 0.7 %copy-done.5 = bf16[96,96]{1,0:T(8,128)(2,1)S(1)} copy-done((bf16[96,96]{1,0:T(8,128)(2,1)S(1)}, bf16[96,96]{1,0:T(8,128)(2,1)}, u32[]{:S(2)}) %copy-start.5) | copy-done | bytes 18456
  6.1 0.0 copy-start.6
  6.1 0.7 %copy-done.6 = s32[48,48]{1,0:T(8,128)S(1)} copy-done((s32[48,48]{1,0:T(8,128)S(1)}, s32[48,48]{1,0:T(8,128)}, u32[]{:S(2)}) %copy-start.6) | copy-done | bytes 9240
  6.8 0.0 copy-start.7
  6.8 0.7 %copy-done.7 = s32[48,48]{1,0:T(8,128)S(1)} copy-done((s32[48,48]{1,0:T(8,128)S(1)}, s32[48,48]{1,0:T(8,128)}, u32[]{:S(2)}) %copy-start.7) | copy-done | bytes 9240
  7.6 21.5 %shard_map.100 = bf16[96,2048]{1,0:T(8,128)(2,1)S(1)} custom-call(s32[16,3]{1,0:T(8,128)S(1)} %copy.11.cols_ref, bf16[192,2048]{1,0:T(8,128)(2,1)S(1)} %bitcast.5, bf16[4,16,3,128,128]{4,3,2,1,0:T(8,128)(2,1)} %t_hbm.1, f32[8,48,48]{2,1,0:T(8,128)S(1)} %copy-done.1, s32[8,48,48]{2,1,0:T(8,128)S(1)} %copy-done.2, bf16[2,48,192]{2,1,0:T(8,128)(2,1)S(1)} %copy-done.4, ...), custom_call_target="tpu_custom_call" | custom-call | tf_op jit(solution)/shard_map/pallas_call | solution.py:283
  29.1 0.7 %copy.13 = bf16[8,12,2048]{2,0,1:T(8,128)(2,1)} copy(bf16[8,12,2048]{2,0,1:T(8,128)(2,1)S(1)} %bitcast.4) | data formatting | bytes 786432
Async XLA Ops:
  0.8 1.1 %copy-start = (bf16[8,24,2048]{2,1,0:T(8,128)(2,1)S(1)}, bf16[8,24,2048]{2,1,0:T(8,128)(2,1)}, u32[]{:S(2)}) copy-start(bf16[8,24,2048]{2,1,0:T(8,128)(2,1)} %param.10) | copy-start | bytes 2359300
  1.9 0.9 %copy-start.1 = (f32[8,48,48]{2,1,0:T(8,128)S(1)}, f32[8,48,48]{2,1,0:T(8,128)}, u32[]{:S(2)}) copy-start(f32[8,48,48]{2,1,0:T(8,128)} %g_hbm.1) | copy-start | bytes 221188
  2.8 0.9 %copy-start.2 = (s32[8,48,48]{2,1,0:T(8,128)S(1)}, s32[8,48,48]{2,1,0:T(8,128)}, u32[]{:S(2)}) copy-start(s32[8,48,48]{2,1,0:T(8,128)} %gm_hbm.1) | copy-start | bytes 221188
  3.7 0.8 %copy-start.3 = (f32[48,192]{1,0:T(8,128)S(1)}, f32[48,192]{1,0:T(8,128)}, u32[]{:S(2)}) copy-start(f32[48,192]{1,0:T(8,128)} %constant.11.clone.same_ref) | copy-start | bytes 110596
  4.5 0.8 %copy-start.4 = (bf16[2,48,192]{2,1,0:T(8,128)(2,1)S(1)}, bf16[2,48,192]{2,1,0:T(8,128)(2,1)}, u32[]{:S(2)}) copy-start(bf16[2,48,192]{2,1,0:T(8,128)(2,1)} %constant.10.clone.spread_ref) | copy-start | bytes 110596
  5.3 0.7 %copy-start.5 = (bf16[96,96]{1,0:T(8,128)(2,1)S(1)}, bf16[96,96]{1,0:T(8,128)(2,1)}, u32[]{:S(2)}) copy-start(bf16[96,96]{1,0:T(8,128)(2,1)} %constant.14.clone.perm_ref) | copy-start | bytes 55300
  6.1 0.7 %copy-start.6 = (s32[48,48]{1,0:T(8,128)S(1)}, s32[48,48]{1,0:T(8,128)}, u32[]{:S(2)}) copy-start(s32[48,48]{1,0:T(8,128)} %constant.13.clone.place_ref) | copy-start | bytes 27652
  6.8 0.7 %copy-start.7 = (s32[48,48]{1,0:T(8,128)S(1)}, s32[48,48]{1,0:T(8,128)}, u32[]{:S(2)}) copy-start(s32[48,48]{1,0:T(8,128)} %constant.12.clone.half_ref) | copy-start | bytes 27652

commit v2 on v1

--- a/solution.py
+++ b/solution.py
@@ -21,8 +21,8 @@
     return fields
 
 
-def kernel(dims, cols_ref, x_hbm, t_hbm, g_hbm, gm_hbm, spread_ref, same_ref, half_ref, place_ref, perm_ref,
-           out_ref, x_all, t_all, g_all, gm_all, mix, z, contrib, part, recv, rim, halo,
+def kernel(dims, cols_hbm, x_hbm, t_hbm, g_hbm, gm_hbm, spread_hbm, same_hbm, half_hbm, place_hbm, perm_hbm,
+           out_ref, cols_ref, spread_ref, same_ref, half_ref, place_ref, perm_ref, x_all, t_all, g_all, gm_all, mix, z, contrib, part, recv, rim, halo,
            local_sem, xs, xr, fs, fr, ys, yr, hs, hr):
     n, space_size, fields, rows_in, own_p, group, modes, block_rows, slots, blk = dims
     chaos = lax.axis_index("chaos")
@@ -42,14 +42,20 @@
     locals_ = [
         pltpu.make_async_copy(g_hbm.at[pl.ds(mode * modes, modes)], g_all, local_sem.at[0]),
         pltpu.make_async_copy(gm_hbm.at[pl.ds(mode * modes, modes)], gm_all, local_sem.at[1]),
-        pltpu.make_async_copy(x_hbm, x_all.at[chaos], local_sem.at[2]),
+        pltpu.make_async_copy(spread_hbm, spread_ref, local_sem.at[2]),
+        pltpu.make_async_copy(same_hbm, same_ref, local_sem.at[3]),
+        pltpu.make_async_copy(half_hbm, half_ref, local_sem.at[4]),
+        pltpu.make_async_copy(place_hbm, place_ref, local_sem.at[5]),
+        pltpu.make_async_copy(perm_hbm, perm_ref, local_sem.at[6]),
+        pltpu.make_async_copy(cols_hbm, cols_ref, local_sem.at[7]),
+        pltpu.make_async_copy(x_hbm, x_all.at[chaos], local_sem.at[8]),
     ]
     for k in range(modes):
         for s in range(slots):
             locals_.append(pltpu.make_async_copy(
                 t_hbm.at[k, :, s],
                 t_all.at[:, pl.ds(k * blk, blk), pl.ds(s * blk, blk)],
-                local_sem.at[3 + k * slots + s],
+                local_sem.at[9 + k * slots + s],
             ))
 
     barrier = pltpu.get_barrier_semaphore()
@@ -111,8 +117,8 @@
 
     lax.fori_loop(0, chunks, start_x, 0)
 
-    locals_[0].wait()
-    locals_[1].wait()
+    for copy in locals_[:8]:
+        copy.wait()
     size_r = 2 * group * own_p
     half = half_ref[...]
     target = (2 * chaos + half * (1 - 2 * mode) + mode) * own_p + place_ref[...]
@@ -130,7 +136,7 @@
                 + jnp.dot(lo, spread_ref[1], preferred_element_type=F32))
         mix[pl.ds(k * size_r, size_r), :] = (both * same_ref[...]).astype(BF16)
     contrib[zero_at] = jnp.zeros((2 * rows, blk), F32)
-    for copy in locals_[2:]:
+    for copy in locals_[8:]:
         copy.wait()
 
     def compute(i):
@@ -172,7 +178,7 @@
                 else:
                     found = zero_at
                     for s in range(1, slots):
-                        offset = lax.rem(cols_ref[rc, s] - (space * block_rows + rc) + shell + REACH, shell) - REACH
+                        offset = lax.rem(cols_ref[s, rc] - (space * block_rows + rc) + shell + REACH, shell) - REACH
                         found = jnp.where(offset == o, rc * slots + s, found)
                 term = contrib[jnp.where(inside, found, zero_at)]
                 total = term if total is None else total + term
@@ -278,14 +284,20 @@
     perm = jnp.asarray((source[:, None] == np.arange(rows)[None, :]).astype(np.float32), BF16)
 
     dims = (n, space_size, fields, rows_in, own_p, group, modes, block_rows, slots, blk)
-    any_ = pl.BlockSpec(memory_space=pl.ANY)
+    hbm = pl.BlockSpec(memory_space=pltpu.HBM)
     vmem = pl.BlockSpec(memory_space=pltpu.VMEM)
     out = pl.pallas_call(
         functools.partial(kernel, dims),
         out_shape=jax.ShapeDtypeStruct((rows, tile), BF16),
-        in_specs=[pl.BlockSpec(memory_space=pltpu.SMEM), any_, any_, any_, any_, vmem, vmem, vmem, vmem, vmem],
+        in_specs=[hbm] * 10,
         out_specs=vmem,
         scratch_shapes=[
+            pltpu.SMEM((slots, block_rows), jnp.int32),
+            pltpu.VMEM(spread.shape, BF16),
+            pltpu.VMEM(same.shape, F32),
+            pltpu.VMEM(half.shape, jnp.int32),
+            pltpu.VMEM(place.shape, jnp.int32),
+            pltpu.VMEM(perm.shape, BF16),
             pltpu.VMEM((n, fields * rows_in, tile), BF16),
             pltpu.VMEM((block_rows, modes * blk, slots * blk), BF16),
             pltpu.VMEM((modes, p_size, p_size), F32),
@@ -297,7 +309,7 @@
             pltpu.VMEM((span, rows, blk), F32),
             pltpu.VMEM((2, REACH, rows, blk), F32),
             pltpu.VMEM((2, REACH, rows, blk), F32),
-            pltpu.SemaphoreType.DMA((3 + modes * slots,)),
+            pltpu.SemaphoreType.DMA((9 + modes * slots,)),
             pltpu.SemaphoreType.DMA((n - 1, chunks)),
             pltpu.SemaphoreType.DMA((n - 1, chunks)),
             pltpu.SemaphoreType.DMA((n - 1, chunks)),
@@ -308,8 +320,8 @@
             pltpu.SemaphoreType.DMA((2,)),
         ],
         compiler_params=pltpu.CompilerParams(
-            collective_id=0, has_side_effects=True, vmem_limit_bytes=48 * 1024 * 1024),
-    )(block_cols, coeffs.reshape(fields * rows_in, tile), tangent, galerkin, galerkin_mask,
+            collective_id=0, has_side_effects=True, vmem_limit_bytes=60 * 1024 * 1024),
+    )(block_cols.T, coeffs.reshape(fields * rows_in, tile), tangent, galerkin, galerkin_mask,
       spread, same, half, place, perm)
     return jnp.transpose(out.reshape(own_p, fields, tile), (1, 0, 2))
 

time: 30.3 us -> 23.7 us (0.78); the launches traced: 29.8 us -> 23.6 us
  local copies, waits for them, and re-layouts: 8.3 us -> 1.77 us
    unnamed x18 -> x1, local copies, waits for them, and re-layouts: 8.3 us -> 1.77 us
where the time goes in v2:
time: 23.7 us; the launch traced here: 23.6 us
  Pallas kernels  21.8 us (92%)
  local copies, waits for them, and re-layouts  1.77 us (7%)
    pallas_call x1, Pallas kernels, per_device(): pl.pallas_call(functools.partial(kernel, dims), out_shape=jax.ShapeDtypeS...  21.8 us
    unnamed x1, local copies, waits for them, and re-layouts  1.77 us

profile of v2, /device:TPU:0, one launch (start us, length us, event | category | flops | bytes accessed | tf_op | source)
XLA Modules:
  0.0 23.6 jit_solution(6587921618900153463)
XLA Ops:
  0.0 21.8 %shard_map.100 = bf16[96,2048]{1,0:T(8,128)(2,1)} custom-call(s32[3,16]{1,0:T(4,128)} %bitcast.7, bf16[192,2048]{1,0:T(8,128)(2,1)} %bitcast.6, bf16[4,16,3,128,128]{4,3,2,1,0:T(8,128)(2,1)} %t_hbm.1, f32[8,48,48]{2,1,0:T(8,128)} %g_hbm.1, s32[8,48,48]{2,1,0:T(8,128)} %gm_hbm.1, bf16[2,48,192]{2,1,0:T(8,128)(2,1)} %constant.10.clone.spread_hbm, ...), custom_call_target="tpu_custom_call" | custom-call | tf_op jit(solution)/shard_map/pallas_call | solution.py:289
  21.8 1.8 %copy.12 = bf16[8,12,2048]{2,0,1:T(8,128)(2,1)} copy(bf16[8,12,2048]{2,0,1:T(8,128)(2,1)} %bitcast.5) | data formatting | bytes 786432

commit v3 on v2

--- a/solution.py
+++ b/solution.py
@@ -51,12 +51,8 @@
         pltpu.make_async_copy(x_hbm, x_all.at[chaos], local_sem.at[8]),
     ]
     for k in range(modes):
-        for s in range(slots):
-            locals_.append(pltpu.make_async_copy(
-                t_hbm.at[k, :, s],
-                t_all.at[:, pl.ds(k * blk, blk), pl.ds(s * blk, blk)],
-                local_sem.at[9 + k * slots + s],
-            ))
+        locals_.append(pltpu.make_async_copy(
+            t_hbm.at[k], t_all.at[:, :, pl.ds(k * blk, blk)], local_sem.at[9 + k]))
 
     barrier = pltpu.get_barrier_semaphore()
     for d in range(1, n):
@@ -159,7 +155,8 @@
                 z[b, 0:2 * rows, k * blk:(k + 1) * blk] = hi[:, b * blk:(b + 1) * blk]
                 z[b, 2 * rows:4 * rows, k * blk:(k + 1) * blk] = lo[:, b * blk:(b + 1) * blk]
         for b in range(2):
-            res = jnp.dot(z[b], t_all[r0 + b], preferred_element_type=F32)
+            right = jnp.concatenate([t_all[r0 + b, s] for s in range(slots)], axis=1)
+            res = jnp.dot(z[b], right, preferred_element_type=F32)
             res = res[:2 * rows] + res[2 * rows:]
             for s in range(slots):
                 contrib[(r0 + b) * slots + s] = res[:, s * blk:(s + 1) * blk]
@@ -285,12 +282,10 @@
 
     dims = (n, space_size, fields, rows_in, own_p, group, modes, block_rows, slots, blk)
     hbm = pl.BlockSpec(memory_space=pltpu.HBM)
-    vmem = pl.BlockSpec(memory_space=pltpu.VMEM)
     out = pl.pallas_call(
         functools.partial(kernel, dims),
-        out_shape=jax.ShapeDtypeStruct((rows, tile), BF16),
+        out_shape=pltpu.VMEM((rows, tile), BF16),
         in_specs=[hbm] * 10,
-        out_specs=vmem,
         scratch_shapes=[
             pltpu.SMEM((slots, block_rows), jnp.int32),
             pltpu.VMEM(spread.shape, BF16),
@@ -299,7 +294,7 @@
             pltpu.VMEM(place.shape, jnp.int32),
             pltpu.VMEM(perm.shape, BF16),
             pltpu.VMEM((n, fields * rows_in, tile), BF16),
-            pltpu.VMEM((block_rows, modes * blk, slots * blk), BF16),
+            pltpu.VMEM((block_rows, slots, modes * blk, blk), BF16),
             pltpu.VMEM((modes, p_size, p_size), F32),
             pltpu.VMEM((modes, p_size, p_size), jnp.int32),
             pltpu.VMEM((modes * size_r, 2 * width), BF16),
@@ -309,7 +304,7 @@
             pltpu.VMEM((span, rows, blk), F32),
             pltpu.VMEM((2, REACH, rows, blk), F32),
             pltpu.VMEM((2, REACH, rows, blk), F32),
-            pltpu.SemaphoreType.DMA((9 + modes * slots,)),
+            pltpu.SemaphoreType.DMA((9 + modes,)),
             pltpu.SemaphoreType.DMA((n - 1, chunks)),
             pltpu.SemaphoreType.DMA((n - 1, chunks)),
             pltpu.SemaphoreType.DMA((n - 1, chunks)),

time: 23.7 us -> 21.9 us (0.924)
  local copies, waits for them, and re-layouts: 1.77 us -> 0.75 us
  Pallas kernels: 21.8 us -> 21 us
    unnamed x1, local copies, waits for them, and re-layouts: 1.77 us -> 0.75 us
    pallas_call x1, Pallas kernels: 21.8 us -> 21 us  [per_device(): pl.pallas_call(functools.partial(kernel, dims), out_shape=pltpu.VMEM((row...]
where the time goes in v3:
time: 21.9 us; the launch traced here: 21.7 us
  Pallas kernels  21 us (96%)
  local copies, waits for them, and re-layouts  0.75 us (3%)
    pallas_call x1, Pallas kernels, per_device(): pl.pallas_call(functools.partial(kernel, dims), out_shape=pltpu.VMEM((row...  21 us
    unnamed x1, local copies, waits for them, and re-layouts  0.75 us

profile of v3, /device:TPU:0, one launch (start us, length us, event | category | flops | bytes accessed | tf_op | source)
XLA Modules:
  0.0 21.7 jit_solution(16461889884972715284)
XLA Ops:
  0.0 21.0 %shard_map.100 = bf16[96,2048]{1,0:T(8,128)(2,1)S(1)} custom-call(s32[3,16]{1,0:T(4,128)} %bitcast.7, bf16[192,2048]{1,0:T(8,128)(2,1)} %bitcast.6, bf16[4,16,3,128,128]{4,3,2,1,0:T(8,128)(2,1)} %t_hbm.1, f32[8,48,48]{2,1,0:T(8,128)} %g_hbm.1, s32[8,48,48]{2,1,0:T(8,128)} %gm_hbm.1, bf16[2,48,192]{2,1,0:T(8,128)(2,1)} %constant.10.clone.spread_hbm, ...), custom_call_target="tpu_custom_call" | custom-call | tf_op jit(solution)/shard_map/pallas_call | solution.py:285
  21.0 0.7 %copy.12 = bf16[8,12,2048]{2,0,1:T(8,128)(2,1)} copy(bf16[8,12,2048]{2,0,1:T(8,128)(2,1)S(1)} %bitcast.5) | data formatting | bytes 786432

commit v4 on v3

--- a/solution.py
+++ b/solution.py
@@ -185,18 +185,23 @@
     def summed(j):
         return part[j, 0:rows] + recv[j]
 
-    def store(column, value):
-        value = jnp.dot(perm_ref[...], value.astype(BF16), preferred_element_type=F32)
+    def store(column, values):
+        value = jnp.concatenate([v.astype(BF16) for v in values], axis=1)
+        value = jnp.dot(perm_ref[...], value, preferred_element_type=F32)
         start = column * blk
         if not isinstance(start, int):
-            start = pl.multiple_of(start, blk)
-        out_ref[:, pl.ds(start, blk)] = value.astype(BF16)
+            start = pl.multiple_of(start, 2 * blk)
+        out_ref[:, pl.ds(start, 2 * blk)] = value.astype(BF16)
 
     def finish(q):
         exchange(q).wait()
         j0 = first_column(q)
-        for e in range(2):
-            store(j0 + e - REACH, summed(j0 + e))
+        store(j0 - REACH, [summed(j0), summed(j0 + 1)])
+
+    def finish_edge(q, side, column):
+        exchange(q).wait()
+        send_rim(side).wait()
+        store(column, [summed(column + REACH + e) + halo[side, e] for e in range(2)])
 
     def finish_rim(q):
         exchange(q).wait()
@@ -206,11 +211,9 @@
         send_rim(q).start()
 
     def step(t, carry):
-        @pl.when(t < chunks)
-        def _():
-            for d in range(1, n):
-                got_x(t, d).wait_recv()
-                forward(t, d, mode).start()
+        for d in range(1, n):
+            got_x(t, d).wait_recv()
+            forward(t, d, mode).start()
 
         @pl.when(t >= 1)
         def _():
@@ -232,19 +235,16 @@
             finish(t - 2)
         return carry
 
-    lax.fori_loop(0, chunks + 1, step, 0)
-    combine(chunks)
-    combine(chunks + 1)
-    for q in range(chunks - 1, chunks + 1):
+    lax.fori_loop(0, chunks, step, 0)
+    finish_edge(2, 0, 0)
+    for d in range(1, n):
+        forward(chunks - 1, d, other).wait_recv()
+    compute(chunks - 1)
+    for q in range(chunks - 1, chunks + 2):
+        combine(q)
+    for q in range(chunks - 2, chunks + 1):
         finish(q)
-    exchange(2).wait()
-    send_rim(0).wait()
-    for e in range(2):
-        store(e, summed(REACH + e) + halo[0, e])
-    exchange(chunks + 1).wait()
-    send_rim(1).wait()
-    for e in range(2):
-        store(block_rows - 2 + e, summed(block_rows + e) + halo[1, e])
+    finish_edge(chunks + 1, 1, block_rows - 2)
 
     def drain(i, carry):
         for d in range(1, n):

time: 21.9 us -> 21.7 us (level)
  no operation moved by 1% of the time
where the time goes in v4:
time: 21.7 us; the launch traced here: 21.6 us
  Pallas kernels  20.8 us (96%)
  local copies, waits for them, and re-layouts  0.75 us (3%)
    pallas_call x1, Pallas kernels, per_device(): pl.pallas_call(functools.partial(kernel, dims), out_shape=pltpu.VMEM((row...  20.8 us
    unnamed x1, local copies, waits for them, and re-layouts  0.75 us

profile of v4, /device:TPU:0, one launch (start us, length us, event | category | flops | bytes accessed | tf_op | source)
XLA Modules:
  0.0 21.6 jit_solution(17391826199594640761)
XLA Ops:
  0.0 20.8 %shard_map.100 = bf16[96,2048]{1,0:T(8,128)(2,1)S(1)} custom-call(s32[3,16]{1,0:T(4,128)} %bitcast.7, bf16[192,2048]{1,0:T(8,128)(2,1)} %bitcast.6, bf16[4,16,3,128,128]{4,3,2,1,0:T(8,128)(2,1)} %t_hbm.1, f32[8,48,48]{2,1,0:T(8,128)} %g_hbm.1, s32[8,48,48]{2,1,0:T(8,128)} %gm_hbm.1, bf16[2,48,192]{2,1,0:T(8,128)(2,1)} %constant.10.clone.spread_hbm, ...), custom_call_target="tpu_custom_call" | custom-call | tf_op jit(solution)/shard_map/pallas_call | solution.py:285
  20.8 0.7 %copy.12 = bf16[8,12,2048]{2,0,1:T(8,128)(2,1)} copy(bf16[8,12,2048]{2,0,1:T(8,128)(2,1)S(1)} %bitcast.5) | data formatting | bytes 786432

commit v5 on v4

--- a/solution.py
+++ b/solution.py
@@ -60,7 +60,7 @@
     pl.semaphore_signal(barrier, inc=1, device_id={"mode": other}, device_id_type=MESH)
     pl.semaphore_signal(barrier, inc=1, device_id={"space": above}, device_id_type=MESH)
     pl.semaphore_signal(barrier, inc=1, device_id={"space": below}, device_id_type=MESH)
-    for copy in locals_:
+    for copy in locals_[:8]:
         copy.start()
     pl.semaphore_wait(barrier, n + 2)
 
@@ -112,6 +112,8 @@
         return carry
 
     lax.fori_loop(0, chunks, start_x, 0)
+    for copy in locals_[8:]:
+        copy.start()
 
     for copy in locals_[:8]:
         copy.wait()
@@ -132,8 +134,6 @@
                 + jnp.dot(lo, spread_ref[1], preferred_element_type=F32))
         mix[pl.ds(k * size_r, size_r), :] = (both * same_ref[...]).astype(BF16)
     contrib[zero_at] = jnp.zeros((2 * rows, blk), F32)
-    for copy in locals_[8:]:
-        copy.wait()
 
     def compute(i):
         r0 = first_row(i)
@@ -214,6 +214,11 @@
         for d in range(1, n):
             got_x(t, d).wait_recv()
             forward(t, d, mode).start()
+
+        @pl.when(t == 1)
+        def _():
+            for copy in locals_[8:]:
+                copy.wait()
 
         @pl.when(t >= 1)
         def _():

time: 21.7 us -> 21.8 us (level)
  no operation moved by 1% of the time
where the time goes in v5:
time: 21.8 us; the launch traced here: 21.6 us
  Pallas kernels  20.8 us (95%)
  local copies, waits for them, and re-layouts  0.75 us (3%)
    pallas_call x1, Pallas kernels, per_device(): pl.pallas_call(functools.partial(kernel, dims), out_shape=pltpu.VMEM((row...  20.8 us
    unnamed x1, local copies, waits for them, and re-layouts  0.75 us

profile of v5, /device:TPU:0, one launch (start us, length us, event | category | flops | bytes accessed | tf_op | source)
XLA Modules:
  0.0 21.6 jit_solution(9982750890350185865)
XLA Ops:
  0.0 20.8 %shard_map.100 = bf16[96,2048]{1,0:T(8,128)(2,1)S(1)} custom-call(s32[3,16]{1,0:T(4,128)} %bitcast.7, bf16[192,2048]{1,0:T(8,128)(2,1)} %bitcast.6, bf16[4,16,3,128,128]{4,3,2,1,0:T(8,128)(2,1)} %t_hbm.1, f32[8,48,48]{2,1,0:T(8,128)} %g_hbm.1, s32[8,48,48]{2,1,0:T(8,128)} %gm_hbm.1, bf16[2,48,192]{2,1,0:T(8,128)(2,1)} %constant.10.clone.spread_hbm, ...), custom_call_target="tpu_custom_call" | custom-call | tf_op jit(solution)/shard_map/pallas_call | solution.py:290
  20.9 0.7 %copy.12 = bf16[8,12,2048]{2,0,1:T(8,128)(2,1)} copy(bf16[8,12,2048]{2,0,1:T(8,128)(2,1)S(1)} %bitcast.5) | data formatting | bytes 786432

commit v6 on v5

--- a/solution.py
+++ b/solution.py
@@ -60,7 +60,7 @@
     pl.semaphore_signal(barrier, inc=1, device_id={"mode": other}, device_id_type=MESH)
     pl.semaphore_signal(barrier, inc=1, device_id={"space": above}, device_id_type=MESH)
     pl.semaphore_signal(barrier, inc=1, device_id={"space": below}, device_id_type=MESH)
-    for copy in locals_[:8]:
+    for copy in locals_[:9]:
         copy.start()
     pl.semaphore_wait(barrier, n + 2)
 
@@ -70,7 +70,7 @@
     def send_x(i, d):
         cols = pl.ds(pl.multiple_of((first_row(i) + mode) * blk, blk), blk)
         return pltpu.make_async_remote_copy(
-            src_ref=x_hbm.at[:, cols], dst_ref=x_all.at[chaos, :, cols],
+            src_ref=x_all.at[chaos, :, cols], dst_ref=x_all.at[chaos, :, cols],
             send_sem=xs.at[d - 1, i], recv_sem=xr.at[d - 1, i],
             device_id={"chaos": lax.rem(chaos + d, n)}, device_id_type=MESH)
 
@@ -78,7 +78,7 @@
         source = lax.rem(chaos + n - d, n)
         cols = pl.ds(pl.multiple_of((first_row(i) + mode) * blk, blk), blk)
         return pltpu.make_async_remote_copy(
-            src_ref=x_hbm.at[:, cols], dst_ref=x_all.at[source, :, cols],
+            src_ref=x_all.at[chaos, :, cols], dst_ref=x_all.at[source, :, cols],
             send_sem=xs.at[d - 1, i], recv_sem=xr.at[d - 1, i],
             device_id={"chaos": lax.rem(chaos + d, n)}, device_id_type=MESH)
 
@@ -111,8 +111,9 @@
             send_x(i, d).start()
         return carry
 
+    locals_[8].wait()
     lax.fori_loop(0, chunks, start_x, 0)
-    for copy in locals_[8:]:
+    for copy in locals_[9:]:
         copy.start()
 
     for copy in locals_[:8]:
@@ -217,7 +218,7 @@
 
         @pl.when(t == 1)
         def _():
-            for copy in locals_[8:]:
+            for copy in locals_[9:]:
                 copy.wait()
 
         @pl.when(t >= 1)

time: 21.8 us -> 21.6 us (level)
  no operation moved by 1% of the time
where the time goes in v6:
time: 21.6 us; the launch traced here: 21.4 us
  Pallas kernels  20.7 us (96%)
  local copies, waits for them, and re-layouts  0.75 us (3%)
    pallas_call x1, Pallas kernels, per_device(): pl.pallas_call(functools.partial(kernel, dims), out_shape=pltpu.VMEM((row...  20.7 us
    unnamed x1, local copies, waits for them, and re-layouts  0.75 us

profile of v6, /device:TPU:0, one launch (start us, length us, event | category | flops | bytes accessed | tf_op | source)
XLA Modules:
  0.0 21.4 jit_solution(533726935047355482)
XLA Ops:
  0.0 20.7 %shard_map.100 = bf16[96,2048]{1,0:T(8,128)(2,1)S(1)} custom-call(s32[3,16]{1,0:T(4,128)} %bitcast.7, bf16[192,2048]{1,0:T(8,128)(2,1)} %bitcast.6, bf16[4,16,3,128,128]{4,3,2,1,0:T(8,128)(2,1)} %t_hbm.1, f32[8,48,48]{2,1,0:T(8,128)} %g_hbm.1, s32[8,48,48]{2,1,0:T(8,128)} %gm_hbm.1, bf16[2,48,192]{2,1,0:T(8,128)(2,1)} %constant.10.clone.spread_hbm, ...), custom_call_target="tpu_custom_call" | custom-call | tf_op jit(solution)/shard_map/pallas_call | solution.py:291
  20.7 0.7 %copy.12 = bf16[8,12,2048]{2,0,1:T(8,128)(2,1)} copy(bf16[8,12,2048]{2,0,1:T(8,128)(2,1)S(1)} %bitcast.5) | data formatting | bytes 786432
